TPU v7x, 32 devices: a whole 2x2x4 slice. The times are simulated.
32 devices in a mesh: dp: 4 (over y, core), seq: 8 (over z, x).
Axes of the slice: x: 2, y: 2, z: 4, core: 2. Of those that a mesh axis runs over, the one named last changes fastest.
Arguments:
- inputs: bfloat16 [4, 1536, 768], P('dp', 'seq'), may hold values from -6 to 6
- cotangent: bfloat16 [4, 1536, 768], P('dp', 'seq'), may hold values from -6 to 6
- dilated_kernel_weight: bfloat16 [768, 3, 384], P('dp'), may hold values from -0.125 to 0.125
- point_weight: bfloat16 [384, 768], P('dp'), may hold values from -0.3125 to 0.3125
Outputs:
- grad_input: bfloat16 [4, 1536, 768], P('dp', 'seq')
- kernel_weight_gradient: float32 [768, 3, 384], P('dp')
- pointwise_weight_gradient: float32 [384, 768], P('dp')
All inputs are finite; a program needn't handle non-finite values.
Results may differ from a plain program's by a relative error of at most 0.0054.
Values may be sent and summed in bfloat16 or wider, within the bound.
A program may use at most 64 MiB of HBM per device.

v0:
```python
import jax
import jax.numpy as jnp
from jax import lax
from jax.sharding import PartitionSpec as P

DILATION_SPAN = 32


def extended(x, sides, width):
    for axis, dim in sides:
        size, length = (lax.axis_size(axis), x.shape[dim])
        up = [(i, (i + 1) % size) for i in range(size - 1)]
        down = [(j, i) for i, j in up]
        last = lax.slice_in_dim(x, length - width, length, axis=dim)
        initial = lax.slice_in_dim(x, 0, width, axis=dim)
        before = lax.ppermute(last, axis, up)
        after = lax.ppermute(initial, axis, down)
        x = jnp.concatenate([before, x, after], axis=dim)
    return x


def gelu_apply(values):
    return jax.nn.gelu(values, approximate=True)


def rms_normed(values):
    return values * lax.rsqrt(jnp.mean(values * values, axis=-1, keepdims=True) + 1e-06)


def conv_forward(padded_activation, weight_full, output_length):
    return sum(
        (
            jnp.einsum(
                "amv,vb->amb",
                padded_activation[
                    :,
                    kernel_tap_index * DILATION_SPAN : kernel_tap_index * DILATION_SPAN
                    + output_length,
                ],
                weight_full[:, kernel_tap_index, :],
                preferred_element_type=jnp.float32,
            )
            for kernel_tap_index in range(3)
        )
    )


def conv_weight_grad(padded_activation, delta_rows, input_length):
    return jnp.stack(
        [
            jnp.einsum(
                "hyr,hyk->rk",
                padded_activation[
                    :,
                    kernel_tap_index * DILATION_SPAN : kernel_tap_index * DILATION_SPAN
                    + input_length,
                ],
                delta_rows,
                preferred_element_type=jnp.float32,
            )
            for kernel_tap_index in range(3)
        ],
        axis=1,
    )


def conv_backward(padded_delta, weight_full, input_length):
    return sum(
        (
            jnp.einsum(
                "mfi,xi->mfx",
                padded_delta[
                    :,
                    (2 - kernel_tap_index) * DILATION_SPAN : (2 - kernel_tap_index) * DILATION_SPAN
                    + input_length,
                ],
                weight_full[:, kernel_tap_index, :],
                preferred_element_type=jnp.float32,
            )
            for kernel_tap_index in range(3)
        )
    )


def per_device(inputs, cotangent, dilated_kernel_weight, point_weight):
    conv_full, pointwise_full_weight = (
        lax.all_gather(dilated_kernel_weight, "dp", axis=0, tiled=True),
        lax.all_gather(point_weight, "dp", axis=0, tiled=True),
    )
    input_length = inputs.shape[1]
    normal, pull_norm = jax.vjp(rms_normed, inputs.astype(jnp.float32))
    activated_hidden, pull_act = jax.vjp(gelu_apply, normal)
    padded_activation = extended(
        activated_hidden.astype(jnp.bfloat16), (("seq", 1),), DILATION_SPAN
    )
    preactivation = conv_forward(padded_activation, conv_full, input_length)
    hidden, pull_hidden = jax.vjp(gelu_apply, preactivation)
    hidden_halfprec = hidden.astype(jnp.bfloat16)
    pointwise_weight_gradient = jnp.einsum(
        "xth,xtr->hr", hidden_halfprec, cotangent, preferred_element_type=jnp.float32
    )
    upstream_gradient = jnp.einsum(
        "pqy,oy->pqo", cotangent, pointwise_full_weight, preferred_element_type=jnp.float32
    )
    delta_rows = pull_hidden(upstream_gradient)[0].astype(jnp.bfloat16)
    kernel_weight_gradient = conv_weight_grad(padded_activation, delta_rows, input_length)
    padded_delta = extended(delta_rows, (("seq", 1),), DILATION_SPAN)
    activation_gradient = conv_backward(padded_delta, conv_full, input_length)
    grad_normal = pull_act(activation_gradient)[0]
    grad_inner = pull_norm(grad_normal)[0]
    grad_input = (cotangent.astype(jnp.float32) + grad_inner).astype(jnp.bfloat16)
    owned_conv, owned_point = (
        lax.psum_scatter(kernel_weight_gradient, "dp", scatter_dimension=0, tiled=True),
        lax.psum_scatter(pointwise_weight_gradient, "dp", scatter_dimension=0, tiled=True),
    )
    owned_conv, owned_point = lax.psum((owned_conv, owned_point), "seq")
    return (grad_input, owned_conv, owned_point)


def solution(mesh):
    return jax.shard_map(
        per_device,
        mesh=mesh,
        in_specs=(P("dp", "seq", None), P("dp", "seq", None), P("dp", None, None), P("dp", None)),
        out_specs=(P("dp", "seq", None), P("dp", None, None), P("dp", None)),
        check_vma=False,
    )
```

profile of v0, /device:TPU:0, one launch (start us, length us, event | category | flops | bytes accessed | tf_op | source)
XLA Modules:
  0.0 200.1 jit_solution(5027804048679086988)
XLA Ops:
  7.2 0.7 all-gather.2.cloned.1.call-update
  7.9 1.1 fusion.19
  9.1 1.3 fusion.16
  10.3 4.8 %collective-permute-start = (bf16[1,32,768]{2,1,0:T(8,128)(2,1)S(1)}, bf16[1,32,768]{2,1,0:T(8,128)(2,1)S(1)}, u32[]{:S(2)}, u32[]{:S(2)}) collective-permute-start(bf16[1,32,768]{2,1,0:T(8,128)(2,1)S(1)} %get-tuple-element.5), channel_id=1, source_target_pairs={{0,1},{1,2},{2,3},{3,4},{4,5},{5,6},{6,7},{8,9},{9,10},{10,11},{11... | collective-permute-start | bytes 147464 | tf_op jit(solution)/shard_map/ppermute | solution.py:16
  15.2 1.3 collective-permute-start.1
  16.5 16.6 %all-gather.2.cloned.1.call-done = bf16[768,3,384]{2,0,1:T(8,128)(2,1)} async-done(((bf16[192,3,384]{2,0,1:T(8,128)(2,1)}), bf16[768,3,384]{2,0,1:T(8,128)(2,1)}) %all-gather.2.cloned.1.call-update) | async-done | bytes 1769488 | tf_op jit(solution)/shard_map/all_gather | solution.py:87
  33.1 1.5 fusion.22
  34.6 1.4 fusion.24
  36.4 1.4 fusion.36
  37.9 7.5 %all_gather.6 = bf16[384,768]{1,0:T(8,128)(2,1)S(1)} all-gather(bf16[96,768]{1,0:T(8,128)(2,1)S(1)} %copy-done.4), channel_id=1, replica_groups=mesh['dp'=4,'seq'=8] {'dp'}, dimensions={0}, use_global_device_ids=true | all-gather | bytes 737280 | tf_op jit(solution)/shard_map/all_gather | solution.py:88
  45.4 0.4 fusion.31
  45.9 0.4 convolution_bitcast_fusion
  46.3 0.4 convolution_bitcast_fusion.2
  46.7 0.4 convolution_bitcast_fusion.1
  47.0 2.0 pad_maximum_fusion
  49.1 1.3 collective-permute-start.2
  50.4 4.6 %collective-permute-start.3 = (bf16[1,32,384]{2,1,0:T(8,128)(2,1)S(1)}, bf16[1,32,384]{2,1,0:T(8,128)(2,1)S(1)}, u32[]{:S(2)}, u32[]{:S(2)}) collective-permute-start(bf16[1,32,384]{2,1,0:T(8,128)(2,1)S(1)} %get-tuple-element.8), channel_id=1, source_target_pairs={{0,1},{1,2},{2,3},{3,4},{4,5},{5,6},{6,7},{8,9},{9,10},{10,11},{11... | collective-permute-start | bytes 73736 | tf_op jit(solution)/shard_map/ppermute | solution.py:16
  55.0 8.7 %reduce-scatter.5.cloned.1.call-done = f32[96,768]{1,0:T(8,128)} async-done(((f32[384,768]{1,0:T(8,128)}), f32[96,768]{1,0:T(8,128)}) %reduce-scatter.5.cloned.1.call-update) | async-done | bytes 294928 | tf_op jit(solution)/shard_map/reduce_scatter | solution.py:114
  63.7 43.2 %reduce-scatter.3.cloned.1.call-done = f32[192,3,384]{2,0,1:T(8,128)} async-done(((f32[768,3,384]{2,0,1:T(8,128)}), f32[192,3,384]{2,0,1:T(8,128)}) %reduce-scatter.3.cloned.1.call-update) | async-done | bytes 884752 | tf_op jit(solution)/shard_map/reduce_scatter | solution.py:113
  107.9 0.8 fusion.20
  108.7 0.9 fusion.12
  109.6 81.0 %all-reduce.3.cloned.1.call-done = (f32[192,3,384]{2,0,1:T(8,128)}, f32[96,768]{1,0:T(8,128)}) async-done(((f32[192,3,384]{2,0,1:T(8,128)}, f32[96,768]{1,0:T(8,128)}), (f32[192,3,384]{2,0,1:T(8,128)}, f32[96,768]{1,0:T(8,128)})) %all-reduce.3.cloned.1.call-update) | async-done | bytes 1179664 | tf_op jit(solution)/shard_map/psum | solution.py:116
  190.6 2.2 %copy.9 = f32[192,3,384]{2,0,1:T(8,128)} copy(f32[192,3,384]{2,0,1:T(8,128)} %get-tuple-element.12) | data formatting | bytes 1769472
  192.8 0.7 copy.10
  (28 shorter events, 1.5 us)
Async XLA Ops:
  7.2 25.9 %all-gather.2.cloned.1.call-start = ((), (), s32[]{:S(2)}) async-start(), calls=%async_computation.2 | async-start | bytes 2211840 | tf_op jit(solution)/shard_map/all_gather | solution.py:87
  7.9 55.8 %reduce-scatter.5.cloned.1.call-start = ((), (), s32[]{:S(2)}) async-start(), calls=%async_computation.4 | async-start | bytes 1474560 | tf_op jit(solution)/shard_map/reduce_scatter | solution.py:114
  10.3 25.7 %collective-permute-start = (bf16[1,32,768]{2,1,0:T(8,128)(2,1)S(1)}, bf16[1,32,768]{2,1,0:T(8,128)(2,1)S(1)}, u32[]{:S(2)}, u32[]{:S(2)}) collective-permute-start(bf16[1,32,768]{2,1,0:T(8,128)(2,1)S(1)} %get-tuple-element.5), channel_id=1, source_target_pairs={{0,1},{1,2},{2,3},{3,4},{4,5},{5,6},{6,7},{8,9},{9,10},{10,11},{11... | collective-permute-start | bytes 147464 | tf_op jit(solution)/shard_map/ppermute | solution.py:16
  15.2 19.4 %collective-permute-start.1 = (bf16[1,32,768]{2,1,0:T(8,128)(2,1)S(1)}, bf16[1,32,768]{2,1,0:T(8,128)(2,1)S(1)}, u32[]{:S(2)}, u32[]{:S(2)}) collective-permute-start(bf16[1,32,768]{2,1,0:T(8,128)(2,1)S(1)} %get-tuple-element.6), channel_id=1, source_target_pairs={{1,0},{2,1},{3,2},{4,3},{5,4},{6,5},{7,6},{9,8},{10,9},{11,10},{12... | collective-permute-start | bytes 147464 | tf_op jit(solution)/shard_map/ppermute | solution.py:17
  33.1 3.0 %copy-start = (bf16[768,3,384]{2,0,1:T(8,128)(2,1)S(1)}, bf16[768,3,384]{2,0,1:T(8,128)(2,1)}, u32[]{:S(2)}) copy-start(bf16[768,3,384]{2,0,1:T(8,128)(2,1)} %all-gather.2.cloned.1.call-done) | copy-start | bytes 5308420
  34.6 1.8 copy-start.2
  36.4 1.5 copy-start.4
  37.8 69.1 %reduce-scatter.3.cloned.1.call-start = ((), (), s32[]{:S(2)}) async-start(), calls=%async_computation.3 | async-start | bytes 4423680 | tf_op jit(solution)/shard_map/reduce_scatter | solution.py:113
  49.1 141.6 %all-reduce.3.cloned.1.call-start = ((), (), s32[]{:S(2)}) async-start(), calls=%async_computation.5 | async-start | bytes 2359296 | tf_op jit(solution)/shard_map/psum | solution.py:116
  49.1 58.5 %collective-permute-start.2 = (bf16[1,32,384]{2,1,0:T(8,128)(2,1)S(1)}, bf16[1,32,384]{2,1,0:T(8,128)(2,1)S(1)}, u32[]{:S(2)}, u32[]{:S(2)}) collective-permute-start(bf16[1,32,384]{2,1,0:T(8,128)(2,1)S(1)} %get-tuple-element.7), channel_id=1, source_target_pairs={{1,0},{2,1},{3,2},{4,3},{5,4},{6,5},{7,6},{9,8},{10,9},{11,10},{12... | collective-permute-start | bytes 73736 | tf_op jit(solution)/shard_map/ppermute | solution.py:17
  50.4 56.9 %collective-permute-start.3 = (bf16[1,32,384]{2,1,0:T(8,128)(2,1)S(1)}, bf16[1,32,384]{2,1,0:T(8,128)(2,1)S(1)}, u32[]{:S(2)}, u32[]{:S(2)}) collective-permute-start(bf16[1,32,384]{2,1,0:T(8,128)(2,1)S(1)} %get-tuple-element.8), channel_id=1, source_target_pairs={{0,1},{1,2},{2,3},{3,4},{4,5},{5,6},{6,7},{8,9},{9,10},{10,11},{11... | collective-permute-start | bytes 73736 | tf_op jit(solution)/shard_map/ppermute | solution.py:16
  106.9 1.0 copy-start.1
  190.6 2.2 %copy-start.3 = (f32[96,768]{1,0:T(8,128)S(1)}, f32[96,768]{1,0:T(8,128)}, u32[]{:S(2)}) copy-start(f32[96,768]{1,0:T(8,128)} %get-tuple-element.13) | copy-start | bytes 884740
Sparse Core Ops, SparseCore 0:
  9.6 23.4 all-gather.1
  38.0 25.7 reduce-scatter.4
  66.4 40.4 reduce-scatter.2
  110.3 80.2 all-reduce.2
where the time goes:
time: 200 us
  waiting for transfers between devices  150 us (75%)
  between operations  13.9 us (7%)
  starting transfers between devices  12.1 us (6%)
  matrix products  7.76 us (4%)
  blocking collectives  7.54 us (4%)
  other arithmetic  5.29 us (3%)
  local copies, waits for them, and re-layouts  3.13 us (2%)
    psum x1, waiting for transfers between devices, per_device(): owned_conv, owned_point = lax.psum((owned_conv, owned_point), 'seq')  81 us
    reduce_scatter x1, waiting for transfers between devices, per_device(): lax.psum_scatter(kernel_weight_gradient, 'dp', scatter_dimension=0, tiled...  43.2 us
    all_gather x1, waiting for transfers between devices, per_device(): lax.all_gather(dilated_kernel_weight, 'dp', axis=0, tiled=True)  16.6 us
    ppermute x2, starting transfers between devices, extended(): before = lax.ppermute(last, axis, up)  9.41 us
    reduce_scatter x1, waiting for transfers between devices, per_device(): lax.psum_scatter(pointwise_weight_gradient, 'dp', scatter_dimension=0, ti...  8.72 us
    all_gather x1, blocking collectives, per_device(): lax.all_gather(point_weight, 'dp', axis=0, tiled=True)  7.54 us
  transfers between devices with their start and end apart: 8, of which 4 were waited for; matrix products, arithmetic and copies ran while one was open for 6% of the time, Pallas kernels for 0%

commit v1 on v0

--- a/solution.py
+++ b/solution.py
@@ -1,9 +1,16 @@
+import functools
+
 import jax
 import jax.numpy as jnp
 from jax import lax
+from jax.experimental import pallas as pl
+from jax.experimental.pallas import tpu as pltpu
 from jax.sharding import PartitionSpec as P
 
 DILATION_SPAN = 32
+MESH = pl.DeviceIdType.MESH
+F32, BF16 = jnp.float32, jnp.bfloat16
+GELU_SCALE, GELU_CUBIC = (2.0 / jnp.pi) ** 0.5, 0.044715
 
 
 def extended(x, sides, width):
@@ -117,9 +124,304 @@
     return (grad_input, owned_conv, owned_point)
 
 
+def gelu_and_slope(v):
+    square = v * v
+    t = jnp.tanh(GELU_SCALE * v * (1.0 + GELU_CUBIC * square))
+    half = 0.5 * (1.0 + t)
+    slope = half + 0.5 * GELU_SCALE * v * (1.0 - t * t) * (1.0 + 3.0 * GELU_CUBIC * square)
+    return v * half, slope
+
+
+def normed(values):
+    scale = lax.rsqrt(jnp.mean(values * values, axis=-1, keepdims=True) + 1e-06)
+    return values * scale, scale
+
+
+def dot(a, b, contract):
+    return lax.dot_general(a, b, (contract, ((), ())), preferred_element_type=F32)
+
+
+NN, NT, TN = ((1,), (0,)), ((1,), (1,)), ((0,), (0,))
+
+
+def fused_kernel(
+    seq,
+    x_ref,
+    cot_ref,
+    wk_ref,
+    wp_ref,
+    gin_ref,
+    grads_ref,
+    weights,
+    x_halo,
+    act,
+    delta,
+    partial,
+    core_out,
+    core_in,
+    y_out,
+    y_in,
+    y_own,
+    x_out,
+    x_in,
+    z_own,
+    z_out,
+    z_in,
+    total,
+    send_sem,
+    recv_sem,
+):
+    span = DILATION_SPAN
+    bins, channels = x_ref.shape
+    pieces, _, ci = weights.shape
+    rows = wk_ref.shape[1]
+    half = rows // 2
+    nz = seq // 2
+    chunk = rows // nz
+    d, s = lax.axis_index("dp"), lax.axis_index("seq")
+    y, c = d // 2, d % 2
+    z, x = s // 2, s % 2
+    sibling = (2 * y + 1 - c, s)
+    across_y = (2 * (1 - y) + c, s)
+    across_x = (d, 2 * z + 1 - x)
+    after, before = (d, (s + 1) % seq), (d, (s + seq - 1) % seq)
+    z_peer = [(z + r) % nz for r in range(1, nz)]
+
+    count = [0]
+    sent = []
+
+    def copy(src, dst, device):
+        i = count[0]
+        count[0] += 1
+        op = pltpu.make_async_remote_copy(
+            src_ref=src,
+            dst_ref=dst,
+            send_sem=send_sem.at[i],
+            recv_sem=recv_sem.at[i],
+            device_id=device,
+            device_id_type=MESH,
+        )
+        op.start()
+        sent.append(op)
+        return op
+
+    def at(start, size, step=16):
+        return pl.ds(pl.multiple_of(start, step), size)
+
+    own = rows * d
+    weights[0, at(own, half), :] = wp_ref[:, :ci]
+    weights[0, at(own + half, half), :] = wp_ref[:, ci:]
+    for k in range(3):
+        weights[1 + k, at(own, rows), :] = wk_ref[k]
+
+    barrier = pltpu.get_barrier_semaphore()
+    peers = [sibling, across_y, across_x, after, before] + [(d, 2 * j + x) for j in z_peer]
+    for device in peers:
+        pl.semaphore_signal(barrier, inc=1, device_id=device, device_id_type=MESH)
+    pl.semaphore_wait(barrier, len(peers))
+
+    def block(g, start, size):
+        return weights.at[2 * g : 2 * g + 2, at(start, size), :]
+
+    def same(ref, device):
+        return copy(ref, ref, device)
+
+    groups = range(pieces // 2)
+    w_y = [same(block(g, own + half * x, half), across_y) for g in groups]
+    halo_after = copy(x_ref.at[bins - span :, :], x_halo.at[0], after)
+    halo_before = copy(x_ref.at[:span, :], x_halo.at[1], before)
+    w_core = [same(block(g, own, rows), sibling) for g in groups]
+
+    normal, _ = normed(x_ref[...].astype(F32))
+    act[span : span + bins, :] = gelu_and_slope(normal)[0].astype(BF16)
+
+    other = rows * (2 * (1 - y) + c)
+    w_x, w_pass = [], []
+    for g in groups:
+        w_y[g].wait_recv()
+        w_x.append(same(block(g, other + half * x, half), across_x))
+        w_pass.append(same(block(g, other + half * x, half), sibling))
+    halo_after.wait_recv()
+    halo_before.wait_recv()
+    for i, edge, start in ((0, 0, 0), (1, seq - 1, span + bins)):
+        side, _ = normed(x_halo[i].astype(F32))
+        side = gelu_and_slope(side)[0]
+        act[start : start + span, :] = jnp.where(s == edge, 0.0, side).astype(BF16)
+    w_last = []
+    for g in groups:
+        w_x[g].wait_recv()
+        w_last.append(same(block(g, other + half * (1 - x), half), sibling))
+    for g in groups:
+        w_core[g].wait_recv()
+        w_pass[g].wait_recv()
+        w_last[g].wait_recv()
+
+    cot = cot_ref[...]
+    preact = sum(dot(act[span * k : span * k + bins, :], weights[1 + k], NN) for k in range(3))
+    hidden, slope = gelu_and_slope(preact)
+    hidden = hidden.astype(BF16)
+
+    def core_step(p):
+        for i in range(2):
+            core_out[p, rows * i : rows * (i + 1), :] = partial[
+                p, at(rows * (2 * i + 1 - c), rows), :
+            ].astype(BF16)
+        return copy(core_out.at[p], core_in.at[p], sibling)
+
+    def y_step(p):
+        core[p].wait_recv()
+        y_out[p] = (
+            partial[p, at(rows * (2 * (1 - y) + c), rows), :]
+            + core_in[p, at(rows * (1 - y), rows), :].astype(F32)
+        ).astype(BF16)
+        op = copy(y_out.at[p], y_in.at[p], across_y)
+        y_own[p] = partial[p, at(own, rows), :] + core_in[p, at(rows * y, rows), :].astype(F32)
+        return op
+
+    def x_step(p):
+        over_y[p].wait_recv()
+        theirs, mine = at(half * (1 - x), half), at(half * x, half)
+        x_out[p] = (y_own[p, theirs, :] + y_in[p, theirs, :].astype(F32)).astype(BF16)
+        op = copy(x_out.at[p], x_in.at[p], across_x)
+        z_own[p] = y_own[p, mine, :] + y_in[p, mine, :].astype(F32)
+        return op
+
+    def z_step(g):
+        for p in (2 * g, 2 * g + 1):
+            over_x[p].wait_recv()
+            z_own[p] = z_own[p] + x_in[p].astype(F32)
+            z_out[p] = z_own[p].astype(BF16)
+        ops = []
+        for r, j in enumerate(z_peer):
+            piece, row = j // (nz // 2), chunk * (j % (nz // 2))
+            ops.append(copy(z_out.at[2 * g + piece, at(row, chunk), :], z_in.at[g, r], (d, 2 * j + x)))
+        return ops
+
+    def spread_z(g):
+        piece, row = 2 * g + z // (nz // 2), chunk * (z % (nz // 2))
+        summed = z_own[piece, at(row, chunk), :]
+        for r in range(nz - 1):
+            over_z[g][r].wait_recv()
+            summed = summed + z_in[g, r].astype(F32)
+        place = total.at[piece, at(half * x + row, chunk), :]
+        place[...] = summed.astype(BF16)
+        return [same(place, (d, 2 * j + x)) for j in z_peer]
+
+    def spread_x(g):
+        for op in spread[g]:
+            op.wait_recv()
+        return same(total.at[2 * g : 2 * g + 2, at(half * x, half), :], across_x)
+
+    core, over_y, over_x, over_z, spread = [], [], [], [], []
+    for i in range(2):
+        product = dot(hidden, cot[:, ci * i : ci * (i + 1)], TN)
+        for owner in range(4):
+            partial[0, rows * owner + half * i : rows * owner + half * (i + 1), :] = product[
+                half * owner : half * (owner + 1)
+            ]
+    core.append(core_step(0))
+
+    wp = weights[0].reshape(4, 2, half, ci)
+    upstream = sum(
+        dot(cot[:, ci * i : ci * (i + 1)], wp[:, i].reshape(4 * half, ci), NT) for i in range(2)
+    )
+    delta[span : span + bins, :] = (upstream * slope).astype(BF16)
+    d_after = copy(delta.at[bins : bins + span, :], delta.at[:span, :], after)
+    d_before = copy(delta.at[span : 2 * span, :], delta.at[span + bins :, :], before)
+    mine = delta[span : span + bins, :]
+    for k in range(3):
+        partial[1 + k] = dot(act[span * k : span * k + bins, :], mine, TN)
+        core.append(core_step(1 + k))
+        over_y.append(y_step(k))
+    over_y.append(y_step(3))
+    over_x.append(x_step(0))
+    over_x.append(x_step(1))
+
+    d_after.wait_recv()
+    d_before.wait_recv()
+    top = jnp.where(s == 0, 0.0, delta[:span, :].astype(F32)).astype(BF16)
+    bottom = jnp.where(s == seq - 1, 0.0, delta[span + bins :, :].astype(F32)).astype(BF16)
+    padded = jnp.concatenate([top, mine, bottom], axis=0)
+    grad = sum(dot(padded[span * (2 - k) : span * (2 - k) + bins], weights[1 + k], NT) for k in range(3))
+    normal, scale = normed(x_ref[...].astype(F32))
+    grad = grad * gelu_and_slope(normal)[1]
+    inner = scale * (grad - normal * jnp.mean(normal * grad, axis=-1, keepdims=True))
+    gin_ref[...] = (cot_ref[...].astype(F32) + inner).astype(BF16)
+
+    over_x.append(x_step(2))
+    over_z.append(z_step(0))
+    over_x.append(x_step(3))
+    spread.append(spread_z(0))
+    over_z.append(z_step(1))
+    last = [spread_x(0)]
+    spread.append(spread_z(1))
+    last.append(spread_x(1))
+    for op in last:
+        op.wait_recv()
+    grads_ref[...] = total[...]
+    for op in sent:
+        op.wait_send()
+
+
+def fused(mesh, inputs, cotangent, dilated_kernel_weight, point_weight):
+    seq = mesh.shape["seq"]
+    nz = seq // 2
+    _, bins, channels = inputs.shape
+    rows, taps, ci = dilated_kernel_weight.shape
+    half, chunk, pieces, owners = rows // 2, rows // nz, taps + 1, mesh.shape["dp"]
+    copies = 5 * (pieces // 2) + 4 + 3 * pieces + (pieces // 2) * (2 * (nz - 1) + 1)
+    grad_input, grads = pl.pallas_call(
+        functools.partial(fused_kernel, seq),
+        out_shape=(
+            jax.ShapeDtypeStruct((bins, channels), BF16),
+            jax.ShapeDtypeStruct((pieces, rows, ci), BF16),
+        ),
+        in_specs=[pl.BlockSpec(memory_space=pltpu.VMEM)] * 4,
+        out_specs=(pl.BlockSpec(memory_space=pltpu.VMEM),) * 2,
+        scratch_shapes=[
+            pltpu.VMEM((pieces, owners * rows, ci), BF16),
+            pltpu.VMEM((2, DILATION_SPAN, channels), BF16),
+            pltpu.VMEM((bins + 2 * DILATION_SPAN, channels), BF16),
+            pltpu.VMEM((bins + 2 * DILATION_SPAN, ci), BF16),
+            pltpu.VMEM((pieces, owners * rows, ci), F32),
+            pltpu.VMEM((pieces, 2 * rows, ci), BF16),
+            pltpu.VMEM((pieces, 2 * rows, ci), BF16),
+            pltpu.VMEM((pieces, rows, ci), BF16),
+            pltpu.VMEM((pieces, rows, ci), BF16),
+            pltpu.VMEM((pieces, rows, ci), F32),
+            pltpu.VMEM((pieces, half, ci), BF16),
+            pltpu.VMEM((pieces, half, ci), BF16),
+            pltpu.VMEM((pieces, half, ci), F32),
+            pltpu.VMEM((pieces, half, ci), BF16),
+            pltpu.VMEM((pieces // 2, nz - 1, chunk, ci), BF16),
+            pltpu.VMEM((pieces, rows, ci), BF16),
+            pltpu.SemaphoreType.DMA((copies,)),
+            pltpu.SemaphoreType.DMA((copies,)),
+        ],
+        compiler_params=pltpu.CompilerParams(
+            collective_id=0, has_side_effects=True, vmem_limit_bytes=48 * 1024 * 1024
+        ),
+    )(inputs[0], cotangent[0], jnp.transpose(dilated_kernel_weight, (1, 0, 2)), point_weight)
+    conv = jnp.transpose(grads[1:], (1, 0, 2)).astype(F32)
+    point = jnp.concatenate([grads[0, :half], grads[0, half:]], axis=1).astype(F32)
+    return grad_input[None], conv, point
+
+
 def solution(mesh):
+    dp, seq = mesh.shape["dp"], mesh.shape["seq"]
+
+    def step(inputs, cotangent, dilated_kernel_weight, point_weight):
+        rows, taps, ci = dilated_kernel_weight.shape
+        nz = seq // 2
+        pairs = dp == 4 and seq % 4 == 0 and inputs.shape[0] == 1 and taps == 3
+        even = rows % 32 == 0 and rows % (16 * nz) == 0
+        shapes = 2 * point_weight.shape[0] == rows and point_weight.shape[1] == 2 * ci
+        if pairs and even and shapes:
+            return fused(mesh, inputs, cotangent, dilated_kernel_weight, point_weight)
+        return per_device(inputs, cotangent, dilated_kernel_weight, point_weight)
+
     return jax.shard_map(
-        per_device,
+        step,
         mesh=mesh,
         in_specs=(P("dp", "seq", None), P("dp", "seq", None), P("dp", None, None), P("dp", None)),
         out_specs=(P("dp", "seq", None), P("dp", None, None), P("dp", None)),

time: 200 us -> 62.5 us (0.31)
  waiting for transfers between devices: 150 us -> 0 us
  Pallas kernels: 0 us -> 55.4 us
  between operations: 13.9 us -> 0.65 us
  starting transfers between devices: 12.1 us -> 0 us
  matrix products: 7.76 us -> 0 us
  blocking collectives: 7.54 us -> 0 us
  other arithmetic: 5.29 us -> 1.71 us
    psum x1 -> x0, waiting for transfers between devices: 81 us -> none  [per_device(): owned_conv, owned_point = lax.psum((owned_conv, owned_point), 'seq')]
    pallas_call x0 -> x1, Pallas kernels: none -> 55.4 us  [fused(): pl.pallas_call(functools.partial(fused_kernel, seq), out_shape=(jax.Shape...]
    reduce_scatter x2 -> x0, waiting for transfers between devices: 51.9 us -> none  [the longest x1 43.2 us: per_device(): lax.psum_scatter(kernel_weight_gradient, 'dp', scatter_dimension=0, tiled...]
    all_gather x1 -> x0, waiting for transfers between devices: 16.6 us -> none  [per_device(): lax.all_gather(dilated_kernel_weight, 'dp', axis=0, tiled=True)]
    ppermute x4 -> x0, starting transfers between devices: 12 us -> none  [the longest x2 9.41 us: extended(): before = lax.ppermute(last, axis, up)]
    dot_general x11 -> x0, matrix products: 7.76 us -> none  [the longest x3 3.23 us: conv_forward(): jnp.einsum('amv,vb->amb', padded_activation[:, kernel_tap_index * DILATIO...]
    all_gather x1 -> x0, blocking collectives: 7.54 us -> none  [per_device(): lax.all_gather(point_weight, 'dp', axis=0, tiled=True)]
    unnamed x12 -> x9, local copies, waits for them, and re-layouts: 3.11 us -> 4.55 us
  transfers between devices with their start and end apart: 8 -> 0, of which waited for: 4 -> 0; matrix products, arithmetic and copies ran while one was open for 6% -> 0% of each run, Pallas kernels for 0% -> 0%
where the time goes in v1:
time: 62.5 us; the launch traced here: 62.3 us
  Pallas kernels  55.4 us (89%)
  local copies, waits for them, and re-layouts  4.57 us (7%)
  other arithmetic  1.71 us (3%)
  between operations  0.65 us (1%)
    pallas_call x1, Pallas kernels, fused(): pl.pallas_call(functools.partial(fused_kernel, seq), out_shape=(jax.Shape...  55.4 us
    unnamed x9, local copies, waits for them, and re-layouts  4.55 us

profile of v1, /device:TPU:0, one launch (start us, length us, event | category | flops | bytes accessed | tf_op | source)
XLA Modules:
  0.0 62.3 jit_solution(16243933389479712089)
XLA Ops:
  0.6 0.0 copy-start
  0.6 1.0 %copy-done = bf16[192,3,384]{2,0,1:T(8,128)(2,1)S(1)} copy-done((bf16[192,3,384]{2,0,1:T(8,128)(2,1)S(1)}, bf16[192,3,384]{2,0,1:T(8,128)(2,1)}, u32[]{:S(2)}) %copy-start) | copy-done | bytes 442392
  1.6 0.0 copy-start.1
  1.6 1.0 %copy-done.1 = bf16[1,192,768]{2,1,0:T(8,128)(2,1)S(1)} copy-done((bf16[1,192,768]{2,1,0:T(8,128)(2,1)S(1)}, bf16[1,192,768]{2,1,0:T(8,128)(2,1)}, u32[]{:S(2)}) %copy-start.1) | copy-done | bytes 294936
  2.6 0.0 copy-start.2
  2.6 1.0 %copy-done.2 = bf16[1,192,768]{2,1,0:T(8,128)(2,1)S(1)} copy-done((bf16[1,192,768]{2,1,0:T(8,128)(2,1)S(1)}, bf16[1,192,768]{2,1,0:T(8,128)(2,1)}, u32[]{:S(2)}) %copy-start.2) | copy-done | bytes 294936
  3.6 0.0 copy-start.3
  3.6 0.9 %copy-done.3 = bf16[96,768]{1,0:T(8,128)(2,1)S(1)} copy-done((bf16[96,768]{1,0:T(8,128)(2,1)S(1)}, bf16[96,768]{1,0:T(8,128)(2,1)}, u32[]{:S(2)}) %copy-start.3) | copy-done | bytes 147480
  4.5 55.4 %shard_map.67 = (bf16[192,768]{1,0:T(8,128)(2,1)S(1)}, bf16[4,192,384]{2,1,0:T(8,128)(2,1)S(1)}) custom-call(bf16[192,768]{1,0:T(8,128)(2,1)S(1)} %bitcast.12, bf16[192,768]{1,0:T(8,128)(2,1)S(1)} %bitcast.13, bf16[3,192,384]{2,1,0:T(8,128)(2,1)S(1)} %bitcast.10, bf16[96,768]{1,0:T(8,128)(2,1)S(1)} %copy-done.3), custom_call_target="tpu_custom_call" | custom-call | tf_op jit(solution)/shard_map/pallas_call | solution.py:373
  59.9 1.0 %convert_bitcast_fusion = f32[192,3,384]{2,0,1:T(8,128)} fusion(bf16[4,192,384]{2,1,0:T(8,128)(2,1)S(1)} %get-tuple-element.6), kind=kLoop, calls=%fused_computation | loop fusion | flops 221184 | bytes 1327104 | tf_op jit(solution)/shard_map/convert_element_type | solution.py:405
  60.8 0.7 %maximum_convert_fusion = f32[96,768]{1,0:T(8,128)} fusion(bf16[96,384]{1,0:T(8,128)(2,1)S(1)} %get-tuple-element.8, bf16[96,384]{1,0:T(8,128)(2,1)S(1)} %get-tuple-element.7), kind=kLoop, calls=%fused_computation.1 | loop fusion | flops 294912 | bytes 442368 | tf_op jit(solution)/shard_map/convert_element_type | solution.py:406
  61.6 0.7 %copy.8 = bf16[1,192,768]{2,1,0:T(8,128)(2,1)} copy(bf16[1,192,768]{2,1,0:T(8,128)(2,1)S(1)} %bitcast.11) | data formatting | bytes 589824
  (1 shorter events, 0.0 us)
Async XLA Ops:
  0.6 1.0 %copy-start = (bf16[192,3,384]{2,0,1:T(8,128)(2,1)S(1)}, bf16[192,3,384]{2,0,1:T(8,128)(2,1)}, u32[]{:S(2)}) copy-start(bf16[192,3,384]{2,0,1:T(8,128)(2,1)} %param.6) | copy-start | bytes 1327108
  1.6 1.0 %copy-start.1 = (bf16[1,192,768]{2,1,0:T(8,128)(2,1)S(1)}, bf16[1,192,768]{2,1,0:T(8,128)(2,1)}, u32[]{:S(2)}) copy-start(bf16[1,192,768]{2,1,0:T(8,128)(2,1)} %param.4) | copy-start | bytes 884740
  2.6 1.0 %copy-start.2 = (bf16[1,192,768]{2,1,0:T(8,128)(2,1)S(1)}, bf16[1,192,768]{2,1,0:T(8,128)(2,1)}, u32[]{:S(2)}) copy-start(bf16[1,192,768]{2,1,0:T(8,128)(2,1)} %param.5) | copy-start | bytes 884740
  3.6 0.9 %copy-start.3 = (bf16[96,768]{1,0:T(8,128)(2,1)S(1)}, bf16[96,768]{1,0:T(8,128)(2,1)}, u32[]{:S(2)}) copy-start(bf16[96,768]{1,0:T(8,128)(2,1)} %wp_ref.1) | copy-start | bytes 442372

commit v2 on v1

--- a/solution.py
+++ b/solution.py
@@ -146,33 +146,38 @@
 
 def fused_kernel(
     seq,
-    x_ref,
-    cot_ref,
+    x_hbm,
+    cot_hbm,
     wk_ref,
     wp_ref,
     gin_ref,
     grads_ref,
     weights,
+    x_ref,
+    cot_ref,
     x_halo,
     act,
+    normal_ref,
+    slope_ref,
     delta,
     partial,
     core_out,
     core_in,
-    y_out,
-    y_in,
-    y_own,
-    x_out,
-    x_in,
+    first_out,
+    first_in,
+    first_own,
+    second_out,
+    second_in,
     z_own,
     z_out,
     z_in,
     total,
+    local_sem,
     send_sem,
     recv_sem,
 ):
     span = DILATION_SPAN
-    bins, channels = x_ref.shape
+    bins, channels = x_hbm.shape
     pieces, _, ci = weights.shape
     rows = wk_ref.shape[1]
     half = rows // 2
@@ -208,56 +213,94 @@
     def at(start, size, step=16):
         return pl.ds(pl.multiple_of(start, step), size)
 
-    own = rows * d
-    weights[0, at(own, half), :] = wp_ref[:, :ci]
-    weights[0, at(own + half, half), :] = wp_ref[:, ci:]
-    for k in range(3):
-        weights[1 + k, at(own, rows), :] = wk_ref[k]
-
     barrier = pltpu.get_barrier_semaphore()
     peers = [sibling, across_y, across_x, after, before] + [(d, 2 * j + x) for j in z_peer]
     for device in peers:
         pl.semaphore_signal(barrier, inc=1, device_id=device, device_id_type=MESH)
+
+    own = rows * d
+    wp_half = [wp_ref.at[:, :ci], wp_ref.at[:, ci:]]
+    local = [
+        (x_hbm, x_ref),
+        (cot_hbm, cot_ref),
+        (wp_half[0], weights.at[0, at(own, half), :]),
+        (wp_half[1], weights.at[0, at(own + half, half), :]),
+        (wk_ref, weights.at[1:, at(own, rows), :]),
+    ]
+    local = [pltpu.make_async_copy(a, b, local_sem.at[i]) for i, (a, b) in enumerate(local)]
+    for op in local:
+        op.start()
     pl.semaphore_wait(barrier, len(peers))
-
-    def block(g, start, size):
-        return weights.at[2 * g : 2 * g + 2, at(start, size), :]
 
     def same(ref, device):
         return copy(ref, ref, device)
 
-    groups = range(pieces // 2)
-    w_y = [same(block(g, own + half * x, half), across_y) for g in groups]
-    halo_after = copy(x_ref.at[bins - span :, :], x_halo.at[0], after)
-    halo_before = copy(x_ref.at[:span, :], x_halo.at[1], before)
-    w_core = [same(block(g, own, rows), sibling) for g in groups]
-
+    def block(p, start, size):
+        return weights.at[p, at(start, size), :]
+
+    mine = block(0, own + half * x, half)
+    w_y = [copy(wp_ref.at[:, at(ci * x, ci, 128)], mine, across_y)]
+    halo_after = copy(x_hbm.at[bins - span :, :], x_halo.at[0], after)
+    halo_before = copy(x_hbm.at[:span, :], x_halo.at[1], before)
+    for k in range(3):
+        mine = block(1 + k, own + half * x, half)
+        w_y.append(copy(wk_ref.at[k, at(half * x, half), :], mine, across_y))
+    w_core = [copy(wp_half[i], block(0, own + half * i, half), sibling) for i in range(2)]
+    w_core.append(copy(wk_ref, weights.at[1:, at(own, rows), :], sibling))
+
+    local[0].wait()
     normal, _ = normed(x_ref[...].astype(F32))
-    act[span : span + bins, :] = gelu_and_slope(normal)[0].astype(BF16)
+    value, slope = gelu_and_slope(normal)
+    act[span : span + bins, :] = value.astype(BF16)
+    normal_ref[...] = normal
+    slope_ref[...] = slope
 
     other = rows * (2 * (1 - y) + c)
-    w_x, w_pass = [], []
-    for g in groups:
-        w_y[g].wait_recv()
-        w_x.append(same(block(g, other + half * x, half), across_x))
-        w_pass.append(same(block(g, other + half * x, half), sibling))
+    w_x, w_pass, w_last = [], [], []
+
+    def pass_y(p):
+        w_y[p].wait_recv()
+        w_x.append(same(block(p, other + half * x, half), across_x))
+        w_pass.append(same(block(p, other + half * x, half), sibling))
+
+    def pass_x(p):
+        w_x[p].wait_recv()
+        w_last.append(same(block(p, other + half * (1 - x), half), sibling))
+
+    def ready(p):
+        w_pass[p].wait_recv()
+        w_last[p].wait_recv()
+
+    pass_y(0)
+    pass_y(1)
     halo_after.wait_recv()
     halo_before.wait_recv()
     for i, edge, start in ((0, 0, 0), (1, seq - 1, span + bins)):
         side, _ = normed(x_halo[i].astype(F32))
         side = gelu_and_slope(side)[0]
         act[start : start + span, :] = jnp.where(s == edge, 0.0, side).astype(BF16)
-    w_last = []
-    for g in groups:
-        w_x[g].wait_recv()
-        w_last.append(same(block(g, other + half * (1 - x), half), sibling))
-    for g in groups:
-        w_core[g].wait_recv()
-        w_pass[g].wait_recv()
-        w_last[g].wait_recv()
-
+    pass_x(0)
+    pass_y(2)
+    pass_x(1)
+    for op in local[1:]:
+        op.wait()
+    for op in w_core:
+        op.wait_recv()
+    pass_y(3)
+    ready(0)
     cot = cot_ref[...]
-    preact = sum(dot(act[span * k : span * k + bins, :], weights[1 + k], NN) for k in range(3))
+    wp = weights[0].reshape(4, 2, half, ci)
+    upstream = sum(
+        dot(cot[:, ci * i : ci * (i + 1)], wp[:, i].reshape(4 * half, ci), NT) for i in range(2)
+    )
+    pass_x(2)
+    ready(1)
+    preact = dot(act[:bins, :], weights[1], NN)
+    pass_x(3)
+    ready(2)
+    preact += dot(act[span : span + bins, :], weights[2], NN)
+    ready(3)
+    preact += dot(act[2 * span : 2 * span + bins, :], weights[3], NN)
     hidden, slope = gelu_and_slope(preact)
     hidden = hidden.astype(BF16)
 
@@ -268,28 +311,38 @@
             ].astype(BF16)
         return copy(core_out.at[p], core_in.at[p], sibling)
 
-    def y_step(p):
+    def first_step(p):
         core[p].wait_recv()
-        y_out[p] = (
-            partial[p, at(rows * (2 * (1 - y) + c), rows), :]
-            + core_in[p, at(rows * (1 - y), rows), :].astype(F32)
-        ).astype(BF16)
-        op = copy(y_out.at[p], y_in.at[p], across_y)
-        y_own[p] = partial[p, at(own, rows), :] + core_in[p, at(rows * y, rows), :].astype(F32)
+        if p % 2 == 0:
+            away, stay = [(2 * (1 - y) + c, 1 - y, 0, rows)], [(d, y, 0, rows)]
+        else:
+            away = [(2 * i + c, i, half * (1 - x), half) for i in range(2)]
+            stay = [(2 * i + c, i, half * x, half) for i in range(2)]
+
+        def summed(owner, slot, row, size):
+            theirs = core_in[p, at(rows * slot + row, size), :].astype(F32)
+            return partial[p, at(rows * owner + row, size), :] + theirs
+
+        for i, part in enumerate(away):
+            first_out[p, part[3] * i : part[3] * (i + 1), :] = summed(*part).astype(BF16)
+        op = copy(first_out.at[p], first_in.at[p], across_x if p % 2 else across_y)
+        for i, part in enumerate(stay):
+            first_own[p, part[3] * i : part[3] * (i + 1), :] = summed(*part)
         return op
 
-    def x_step(p):
-        over_y[p].wait_recv()
-        theirs, mine = at(half * (1 - x), half), at(half * x, half)
-        x_out[p] = (y_own[p, theirs, :] + y_in[p, theirs, :].astype(F32)).astype(BF16)
-        op = copy(x_out.at[p], x_in.at[p], across_x)
-        z_own[p] = y_own[p, mine, :] + y_in[p, mine, :].astype(F32)
+    def second_step(p):
+        first[p].wait_recv()
+        side, device = (y, across_y) if p % 2 else (x, across_x)
+        theirs, ours = at(half * (1 - side), half), at(half * side, half)
+        second_out[p] = (first_own[p, theirs, :] + first_in[p, theirs, :].astype(F32)).astype(BF16)
+        op = copy(second_out.at[p], second_in.at[p], device)
+        z_own[p] = first_own[p, ours, :] + first_in[p, ours, :].astype(F32)
         return op
 
     def z_step(g):
         for p in (2 * g, 2 * g + 1):
-            over_x[p].wait_recv()
-            z_own[p] = z_own[p] + x_in[p].astype(F32)
+            second[p].wait_recv()
+            z_own[p] = z_own[p] + second_in[p].astype(F32)
             z_out[p] = z_own[p].astype(BF16)
         ops = []
         for r, j in enumerate(z_peer):
@@ -305,14 +358,18 @@
             summed = summed + z_in[g, r].astype(F32)
         place = total.at[piece, at(half * x + row, chunk), :]
         place[...] = summed.astype(BF16)
-        return [same(place, (d, 2 * j + x)) for j in z_peer]
+        ops = [same(place, (d, 2 * j + x)) for j in z_peer]
+        last.append(same(place, across_x))
+        return ops
 
     def spread_x(g):
-        for op in spread[g]:
-            op.wait_recv()
-        return same(total.at[2 * g : 2 * g + 2, at(half * x, half), :], across_x)
-
-    core, over_y, over_x, over_z, spread = [], [], [], [], []
+        for r in range(1, nz):
+            spread[g][r - 1].wait_recv()
+            j = (z + nz - r) % nz
+            piece, row = 2 * g + j // (nz // 2), chunk * (j % (nz // 2))
+            last.append(same(total.at[piece, at(half * x + row, chunk), :], across_x))
+
+    core, first, second, over_z, spread, last = [], [], [], [], [], []
     for i in range(2):
         product = dot(hidden, cot[:, ci * i : ci * (i + 1)], TN)
         for owner in range(4):
@@ -321,10 +378,6 @@
             ]
     core.append(core_step(0))
 
-    wp = weights[0].reshape(4, 2, half, ci)
-    upstream = sum(
-        dot(cot[:, ci * i : ci * (i + 1)], wp[:, i].reshape(4 * half, ci), NT) for i in range(2)
-    )
     delta[span : span + bins, :] = (upstream * slope).astype(BF16)
     d_after = copy(delta.at[bins : bins + span, :], delta.at[:span, :], after)
     d_before = copy(delta.at[span : 2 * span, :], delta.at[span + bins :, :], before)
@@ -332,10 +385,8 @@
     for k in range(3):
         partial[1 + k] = dot(act[span * k : span * k + bins, :], mine, TN)
         core.append(core_step(1 + k))
-        over_y.append(y_step(k))
-    over_y.append(y_step(3))
-    over_x.append(x_step(0))
-    over_x.append(x_step(1))
+        first.append(first_step(k))
+    first.append(first_step(3))
 
     d_after.wait_recv()
     d_before.wait_recv()
@@ -343,19 +394,22 @@
     bottom = jnp.where(s == seq - 1, 0.0, delta[span + bins :, :].astype(F32)).astype(BF16)
     padded = jnp.concatenate([top, mine, bottom], axis=0)
     grad = sum(dot(padded[span * (2 - k) : span * (2 - k) + bins], weights[1 + k], NT) for k in range(3))
-    normal, scale = normed(x_ref[...].astype(F32))
-    grad = grad * gelu_and_slope(normal)[1]
+    second.append(second_step(0))
+    second.append(second_step(1))
+    normal = normal_ref[...]
+    _, scale = normed(x_ref[...].astype(F32))
+    grad = grad * slope_ref[...]
     inner = scale * (grad - normal * jnp.mean(normal * grad, axis=-1, keepdims=True))
     gin_ref[...] = (cot_ref[...].astype(F32) + inner).astype(BF16)
 
-    over_x.append(x_step(2))
     over_z.append(z_step(0))
-    over_x.append(x_step(3))
+    second.append(second_step(2))
+    second.append(second_step(3))
     spread.append(spread_z(0))
     over_z.append(z_step(1))
-    last = [spread_x(0)]
+    spread_x(0)
     spread.append(spread_z(1))
-    last.append(spread_x(1))
+    spread_x(1)
     for op in last:
         op.wait_recv()
     grads_ref[...] = total[...]
@@ -369,19 +423,23 @@
     _, bins, channels = inputs.shape
     rows, taps, ci = dilated_kernel_weight.shape
     half, chunk, pieces, owners = rows // 2, rows // nz, taps + 1, mesh.shape["dp"]
-    copies = 5 * (pieces // 2) + 4 + 3 * pieces + (pieces // 2) * (2 * (nz - 1) + 1)
+    copies = 4 * pieces + 3 + 4 + 3 * pieces + (pieces // 2) * (3 * nz - 2)
     grad_input, grads = pl.pallas_call(
         functools.partial(fused_kernel, seq),
         out_shape=(
             jax.ShapeDtypeStruct((bins, channels), BF16),
             jax.ShapeDtypeStruct((pieces, rows, ci), BF16),
         ),
-        in_specs=[pl.BlockSpec(memory_space=pltpu.VMEM)] * 4,
+        in_specs=[pl.BlockSpec(memory_space=pltpu.HBM)] * 4,
         out_specs=(pl.BlockSpec(memory_space=pltpu.VMEM),) * 2,
         scratch_shapes=[
             pltpu.VMEM((pieces, owners * rows, ci), BF16),
+            pltpu.VMEM((bins, channels), BF16),
+            pltpu.VMEM((bins, channels), BF16),
             pltpu.VMEM((2, DILATION_SPAN, channels), BF16),
             pltpu.VMEM((bins + 2 * DILATION_SPAN, channels), BF16),
+            pltpu.VMEM((bins, channels), F32),
+            pltpu.VMEM((bins, channels), F32),
             pltpu.VMEM((bins + 2 * DILATION_SPAN, ci), BF16),
             pltpu.VMEM((pieces, owners * rows, ci), F32),
             pltpu.VMEM((pieces, 2 * rows, ci), BF16),
@@ -395,6 +453,7 @@
             pltpu.VMEM((pieces, half, ci), BF16),
             pltpu.VMEM((pieces // 2, nz - 1, chunk, ci), BF16),
             pltpu.VMEM((pieces, rows, ci), BF16),
+            pltpu.SemaphoreType.DMA((5,)),
             pltpu.SemaphoreType.DMA((copies,)),
             pltpu.SemaphoreType.DMA((copies,)),
         ],

time: 62.5 us -> 61.3 us (0.981)
  Pallas kernels: 55.4 us -> 54.2 us
    pallas_call x1, Pallas kernels: 55.4 us -> 54.2 us  [fused(): pl.pallas_call(functools.partial(fused_kernel, seq), out_shape=(jax.Shape...]
where the time goes in v2:
time: 61.3 us; the launch traced here: 61.1 us
  Pallas kernels  54.2 us (88%)
  local copies, waits for them, and re-layouts  4.57 us (7%)
  other arithmetic  1.71 us (3%)
  between operations  0.65 us (1%)
    pallas_call x1, Pallas kernels, fused(): pl.pallas_call(functools.partial(fused_kernel, seq), out_shape=(jax.Shape...  54.2 us
    unnamed x9, local copies, waits for them, and re-layouts  4.55 us

profile of v2, /device:TPU:0, one launch (start us, length us, event | category | flops | bytes accessed | tf_op | source)
XLA Modules:
  0.0 61.1 jit_solution(13930827339094065368)
XLA Ops:
  0.6 0.0 copy-start
  0.6 1.0 %copy-done = bf16[192,3,384]{2,0,1:T(8,128)(2,1)S(1)} copy-done((bf16[192,3,384]{2,0,1:T(8,128)(2,1)S(1)}, bf16[192,3,384]{2,0,1:T(8,128)(2,1)}, u32[]{:S(2)}) %copy-start) | copy-done | bytes 442392
  1.6 0.0 copy-start.1
  1.6 1.0 %copy-done.1 = bf16[1,192,768]{2,1,0:T(8,128)(2,1)S(1)} copy-done((bf16[1,192,768]{2,1,0:T(8,128)(2,1)S(1)}, bf16[1,192,768]{2,1,0:T(8,128)(2,1)}, u32[]{:S(2)}) %copy-start.1) | copy-done | bytes 294936
  2.6 0.0 copy-start.2
  2.6 1.0 %copy-done.2 = bf16[1,192,768]{2,1,0:T(8,128)(2,1)S(1)} copy-done((bf16[1,192,768]{2,1,0:T(8,128)(2,1)S(1)}, bf16[1,192,768]{2,1,0:T(8,128)(2,1)}, u32[]{:S(2)}) %copy-start.2) | copy-done | bytes 294936
  3.6 0.0 copy-start.3
  3.6 0.9 %copy-done.3 = bf16[96,768]{1,0:T(8,128)(2,1)S(1)} copy-done((bf16[96,768]{1,0:T(8,128)(2,1)S(1)}, bf16[96,768]{1,0:T(8,128)(2,1)}, u32[]{:S(2)}) %copy-start.3) | copy-done | bytes 147480
  4.5 54.2 %shard_map.67 = (bf16[192,768]{1,0:T(8,128)(2,1)S(1)}, bf16[4,192,384]{2,1,0:T(8,128)(2,1)S(1)}) custom-call(bf16[192,768]{1,0:T(8,128)(2,1)S(1)} %bitcast.12, bf16[192,768]{1,0:T(8,128)(2,1)S(1)} %bitcast.13, bf16[3,192,384]{2,1,0:T(8,128)(2,1)S(1)} %bitcast.10, bf16[96,768]{1,0:T(8,128)(2,1)S(1)} %copy-done.3), custom_call_target="tpu_custom_call" | custom-call | tf_op jit(solution)/shard_map/pallas_call | solution.py:427
  58.6 1.0 %convert_bitcast_fusion = f32[192,3,384]{2,0,1:T(8,128)} fusion(bf16[4,192,384]{2,1,0:T(8,128)(2,1)S(1)} %get-tuple-element.6), kind=kLoop, calls=%fused_computation | loop fusion | flops 221184 | bytes 1327104 | tf_op jit(solution)/shard_map/convert_element_type | solution.py:464
  59.6 0.7 %maximum_convert_fusion = f32[96,768]{1,0:T(8,128)} fusion(bf16[96,384]{1,0:T(8,128)(2,1)S(1)} %get-tuple-element.8, bf16[96,384]{1,0:T(8,128)(2,1)S(1)} %get-tuple-element.7), kind=kLoop, calls=%fused_computation.1 | loop fusion | flops 294912 | bytes 442368 | tf_op jit(solution)/shard_map/convert_element_type | solution.py:465
  60.4 0.7 %copy.8 = bf16[1,192,768]{2,1,0:T(8,128)(2,1)} copy(bf16[1,192,768]{2,1,0:T(8,128)(2,1)S(1)} %bitcast.11) | data formatting | bytes 589824
  (1 shorter events, 0.0 us)
Async XLA Ops:
  0.6 1.0 %copy-start = (bf16[192,3,384]{2,0,1:T(8,128)(2,1)S(1)}, bf16[192,3,384]{2,0,1:T(8,128)(2,1)}, u32[]{:S(2)}) copy-start(bf16[192,3,384]{2,0,1:T(8,128)(2,1)} %param.6) | copy-start | bytes 1327108
  1.6 1.0 %copy-start.1 = (bf16[1,192,768]{2,1,0:T(8,128)(2,1)S(1)}, bf16[1,192,768]{2,1,0:T(8,128)(2,1)}, u32[]{:S(2)}) copy-start(bf16[1,192,768]{2,1,0:T(8,128)(2,1)} %param.4) | copy-start | bytes 884740
  2.6 1.0 %copy-start.2 = (bf16[1,192,768]{2,1,0:T(8,128)(2,1)S(1)}, bf16[1,192,768]{2,1,0:T(8,128)(2,1)}, u32[]{:S(2)}) copy-start(bf16[1,192,768]{2,1,0:T(8,128)(2,1)} %param.5) | copy-start | bytes 884740
  3.6 0.9 %copy-start.3 = (bf16[96,768]{1,0:T(8,128)(2,1)S(1)}, bf16[96,768]{1,0:T(8,128)(2,1)}, u32[]{:S(2)}) copy-start(bf16[96,768]{1,0:T(8,128)(2,1)} %wp_ref.1) | copy-start | bytes 442372

commit v3 on v2

--- a/solution.py
+++ b/solution.py
@@ -458,7 +458,7 @@
             pltpu.SemaphoreType.DMA((copies,)),
         ],
         compiler_params=pltpu.CompilerParams(
-            collective_id=0, has_side_effects=True, vmem_limit_bytes=48 * 1024 * 1024
+            collective_id=0, has_side_effects=True, vmem_limit_bytes=63 * 1024 * 1024
         ),
     )(inputs[0], cotangent[0], jnp.transpose(dilated_kernel_weight, (1, 0, 2)), point_weight)
     conv = jnp.transpose(grads[1:], (1, 0, 2)).astype(F32)

time: 61.3 us -> 60.9 us (level)
  local copies, waits for them, and re-layouts: 4.57 us -> 1.96 us
  Pallas kernels: 54.2 us -> 55.3 us
  other arithmetic: 1.71 us -> 2.72 us
    unnamed x9 -> x3, local copies, waits for them, and re-layouts: 4.55 us -> 1.03 us
    pallas_call x1, Pallas kernels: 54.2 us -> 55.3 us  [fused(): pl.pallas_call(functools.partial(fused_kernel, seq), out_shape=(jax.Shape...]
    convert_element_type x1, other arithmetic: 0.97 us -> 1.98 us  [fused(): conv = jnp.transpose(grads[1:], (1, 0, 2)).astype(F32)]
    squeeze x1, local copies, waits for them, and re-layouts: 0.02 us -> 0.94 us  [fused(): grads[0, :half]]
where the time goes in v3:
time: 60.9 us; the launch traced here: 60.6 us
  Pallas kernels  55.3 us (91%)
  other arithmetic  2.72 us (4%)
  local copies, waits for them, and re-layouts  1.96 us (3%)
  between operations  0.65 us (1%)
    pallas_call x1, Pallas kernels, fused(): pl.pallas_call(functools.partial(fused_kernel, seq), out_shape=(jax.Shape...  55.3 us
    convert_element_type x1, other arithmetic, fused(): conv = jnp.transpose(grads[1:], (1, 0, 2)).astype(F32)  1.98 us

profile of v3, /device:TPU:0, one launch (start us, length us, event | category | flops | bytes accessed | tf_op | source)
XLA Modules:
  0.0 60.6 jit_solution(15556085852378545418)
XLA Ops:
  0.6 55.3 %shard_map.67 = (bf16[192,768]{1,0:T(8,128)(2,1)}, bf16[4,192,384]{2,1,0:T(8,128)(2,1)}) custom-call(bf16[192,768]{1,0:T(8,128)(2,1)} %bitcast.12, bf16[192,768]{1,0:T(8,128)(2,1)} %bitcast.13, bf16[3,192,384]{2,1,0:T(8,128)(2,1)} %bitcast.10, bf16[96,768]{1,0:T(8,128)(2,1)} %wp_ref.1), custom_call_target="tpu_custom_call" | custom-call | tf_op jit(solution)/shard_map/pallas_call | solution.py:427
  55.9 2.0 %convert_bitcast_fusion = f32[192,3,384]{2,0,1:T(8,128)} fusion(bf16[4,192,384]{2,1,0:T(8,128)(2,1)} %get-tuple-element.6), kind=kLoop, calls=%fused_computation | loop fusion | flops 221184 | bytes 1327104 | tf_op jit(solution)/shard_map/convert_element_type | solution.py:464
  57.9 0.9 %slice_bitcast_fusion.1 = (bf16[96,384]{1,0:T(8,128)(2,1)S(1)}, bf16[96,384]{1,0:T(8,128)(2,1)S(1)}) fusion(bf16[4,192,384]{2,1,0:T(8,128)(2,1)} %get-tuple-element.6), kind=kLoop, calls=%fused_computation.3 | loop fusion | bytes 294912 | tf_op jit(solution)/shard_map/squeeze | solution.py:465
  58.9 0.0 copy-start
  58.9 0.7 %maximum_convert_fusion = f32[96,768]{1,0:T(8,128)} fusion(bf16[96,384]{1,0:T(8,128)(2,1)S(1)} %get-tuple-element.8, bf16[96,384]{1,0:T(8,128)(2,1)S(1)} %get-tuple-element.7), kind=kLoop, calls=%fused_computation.1 | loop fusion | flops 294912 | bytes 442368 | tf_op jit(solution)/shard_map/convert_element_type | solution.py:465
  59.6 0.3 copy-done
  59.9 0.7 %copy.8 = bf16[1,192,768]{2,1,0:T(8,128)(2,1)} copy(bf16[1,192,768]{2,1,0:T(8,128)(2,1)S(1)} %bitcast.11) | data formatting | bytes 589824
Async XLA Ops:
  58.9 1.1 %copy-start = (bf16[192,768]{1,0:T(8,128)(2,1)S(1)}, bf16[192,768]{1,0:T(8,128)(2,1)}, u32[]{:S(2)}) copy-start(bf16[192,768]{1,0:T(8,128)(2,1)} %get-tuple-element.5) | copy-start | bytes 884740
